TPU v7x, 32 devices: a whole 2x2x4 slice. The times are simulated.
32 devices in a mesh: dp: 8 (over z, x), walk: 4 (over y, core).
Axes of the slice: x: 2, y: 2, z: 4, core: 2. Of those that a mesh axis runs over, the one named last changes fastest.
Arguments:
- fields: float32 [512, 65536], P('walk', 'dp'), may hold values from -6 to 6
- sensitivity: bfloat16 [256, 16, 128, 128], P('dp'), may hold values from -0.125 to 0.125
- tile_index: int32 [256, 16], P('dp'), may hold values from 0 to 511
- tile_count: int32 [256], P('dp'), may hold values from 1 to 16, as said below
- observed: float32 [32768], P('dp'), may hold values from -6 to 6
- precision: float32 [32768], P('dp'), may hold values from 0.2 to 4
Outputs:
- fields_next: float32 [512, 65536], P('walk', 'dp')
Inputs may be any that keep to these rules, and one draw needn't show every extreme that they name: `tile_count`: every block of rows uses between 1 and 16 slots, and some block uses all 16; slots at or past the count are ignored.
All inputs are finite; a program needn't handle non-finite values.
Results may differ from a plain program's by a relative error of at most 0.0023.
Values may be sent and summed in bfloat16 or wider, within the bound.
A program may use at most 128 MiB of HBM per device.

v0:
```python
import jax
import jax.numpy as jnp
from jax import lax
from jax.sharding import PartitionSpec as P

WALKERS = 512


def forward(gathered, sensitivity, tile_index, tile_count):
    walkers_here = gathered.shape[0]
    nblocks = sensitivity.shape[0]
    tile_rows = sensitivity.shape[2]
    cell_blocks = gathered.reshape(walkers_here, -1, tile_rows)
    most_live = jnp.max(tile_count)

    def one_slot(slot_id, totals):
        columns = lax.dynamic_index_in_dim(tile_index, slot_id, 1, keepdims=False)
        blocks = jnp.take(cell_blocks, columns, axis=1)
        sensitive = lax.dynamic_index_in_dim(sensitivity, slot_id, 1, keepdims=False)
        product = jnp.einsum("brc,wbc->wbr", sensitive, blocks, preferred_element_type=jnp.float32)
        alive_mask = (slot_id < tile_count)[None, :, None]
        return totals + jnp.where(alive_mask, product, jnp.float32(0.0))

    start_sum = jnp.zeros((walkers_here, nblocks, tile_rows), jnp.float32)
    totals = lax.fori_loop(0, most_live, one_slot, start_sum)
    return totals.reshape(walkers_here, nblocks * tile_rows)


def local(fields, sensitivity, tile_index, tile_count, observed, precision):
    field_bf = fields.astype(jnp.bfloat16)
    gathered = lax.all_gather(field_bf, "dp", axis=1, tiled=True)
    predicted = forward(gathered, sensitivity, tile_index, tile_count)
    pred_sum = lax.psum(jnp.sum(predicted, axis=0), "walk")
    pred_mean = pred_sum / WALKERS
    deviation = (predicted - pred_mean[None, :]).astype(jnp.bfloat16)
    misfit = (precision[None, :] * (predicted - observed[None, :])).astype(jnp.bfloat16)
    partial_rows = lax.dot_general(
        misfit,
        lax.all_gather(deviation, "walk", axis=0, tiled=True),
        (((1,), (1,)), ((), ())),
        preferred_element_type=jnp.float32,
    )
    coupling_mine = lax.psum(partial_rows, "dp") / WALKERS
    squares = lax.psum(jnp.sum(coupling_mine * coupling_mine), "walk")
    spread = jnp.sqrt(squares / (WALKERS * WALKERS) + 1e-06)
    weights = (8.0 * coupling_mine / (WALKERS * spread)).astype(jnp.bfloat16)
    update = jnp.dot(
        weights,
        lax.all_gather(field_bf, "walk", axis=0, tiled=True),
        preferred_element_type=jnp.float32,
    )
    return fields - update


def solution(mesh):
    placed = (P("walk", "dp"), P("dp", None, None, None), P("dp", None), P("dp"), P("dp"), P("dp"))
    return jax.shard_map(
        local, mesh=mesh, in_specs=placed, out_specs=P("walk", "dp"), check_vma=False
    )
```

profile of v0, /device:TPU:0, one launch (start us, length us, event | category | flops | bytes accessed | tf_op | source)
XLA Modules:
  0.0 632.2 jit_solution(5999888927857076047)
XLA Ops:
  6.5 4.6 copy.11
  11.9 229.7 %all-gather.4.cloned.1.call-done = bf16[128,65536]{0,1:T(8,128)(2,1)} async-done(((bf16[128,8192]{0,1:T(8,128)(2,1)}), bf16[128,65536]{0,1:T(8,128)(2,1)}) %all-gather.4.cloned.1.call-update) | async-done | bytes 16777232 | tf_op jit(solution)/shard_map/all_gather | solution.py:31
  241.7 22.4 %copy.12 = bf16[128,512,128]{2,0,1:T(8,128)(2,1)} copy(bf16[128,512,128]{0,2,1:T(8,128)(2,1)} %bitcast.37) | data formatting | bytes 33554432 | tf_op jit(solution)/shard_map/while | solution.py:25
  264.3 167.2 %while.10 = (s32[]{:T(128)}, f32[128,32,128]{2,0,1:T(8,128)S(1)}, s32[]{:T(128)}, s32[32]{0:T(128)S(1)}, s32[32,16]{0,1:T(8,128)}, /*index=5*/bf16[128,512,128]{...) while((s32[]{:T(128)}, f32[128,32,128]{2,0,1:T(8,128)S(1)}, ...), condition=%wide.region_2.3_spmd, body=%wide.region_1.2_spmd.sunk | while | flops 135791840 | bytes 8393619 | solution.py:25
  265.6 6.5 %gather_fusion = bf16[32,128,128]{2,1,0:T(8,128)(2,1)S(1)} fusion(bf16[128,512,128]{2,0,1:T(8,128)(2,1)} %get-tuple-element.156, s32[1024]{0:T(1024)S(1)} %pad_clamp_fusion.2), kind=kCustom, calls=%fused_computation.clone.1 | custom fusion | bytes 2097280 | tf_op jit(solution)/shard_map/while/body/jit(_take)/gather | solution.py:18
  272.2 2.5 bitcast_add_fusion.2
  276.1 6.5 %gather_fusion = bf16[32,128,128]{2,1,0:T(8,128)(2,1)S(1)} fusion(bf16[128,512,128]{2,0,1:T(8,128)(2,1)} %get-tuple-element.156, s32[1024]{0:T(1024)S(1)} %pad_clamp_fusion.2), kind=kCustom, calls=%fused_computation.clone.1 | custom fusion | bytes 2097280 | tf_op jit(solution)/shard_map/while/body/jit(_take)/gather | solution.py:18
  282.6 2.5 bitcast_add_fusion.2
  286.5 6.5 %gather_fusion = bf16[32,128,128]{2,1,0:T(8,128)(2,1)S(1)} fusion(bf16[128,512,128]{2,0,1:T(8,128)(2,1)} %get-tuple-element.156, s32[1024]{0:T(1024)S(1)} %pad_clamp_fusion.2), kind=kCustom, calls=%fused_computation.clone.1 | custom fusion | bytes 2097280 | tf_op jit(solution)/shard_map/while/body/jit(_take)/gather | solution.py:18
  293.0 2.5 bitcast_add_fusion.2
  296.9 6.5 %gather_fusion = bf16[32,128,128]{2,1,0:T(8,128)(2,1)S(1)} fusion(bf16[128,512,128]{2,0,1:T(8,128)(2,1)} %get-tuple-element.156, s32[1024]{0:T(1024)S(1)} %pad_clamp_fusion.2), kind=kCustom, calls=%fused_computation.clone.1 | custom fusion | bytes 2097280 | tf_op jit(solution)/shard_map/while/body/jit(_take)/gather | solution.py:18
  303.4 2.5 bitcast_add_fusion.2
  307.3 6.5 %gather_fusion = bf16[32,128,128]{2,1,0:T(8,128)(2,1)S(1)} fusion(bf16[128,512,128]{2,0,1:T(8,128)(2,1)} %get-tuple-element.156, s32[1024]{0:T(1024)S(1)} %pad_clamp_fusion.2), kind=kCustom, calls=%fused_computation.clone.1 | custom fusion | bytes 2097280 | tf_op jit(solution)/shard_map/while/body/jit(_take)/gather | solution.py:18
  317.7 6.5 %gather_fusion = bf16[32,128,128]{2,1,0:T(8,128)(2,1)S(1)} fusion(bf16[128,512,128]{2,0,1:T(8,128)(2,1)} %get-tuple-element.156, s32[1024]{0:T(1024)S(1)} %pad_clamp_fusion.2), kind=kCustom, calls=%fused_computation.clone.1 | custom fusion | bytes 2097280 | tf_op jit(solution)/shard_map/while/body/jit(_take)/gather | solution.py:18
  328.1 6.5 %gather_fusion = bf16[32,128,128]{2,1,0:T(8,128)(2,1)S(1)} fusion(bf16[128,512,128]{2,0,1:T(8,128)(2,1)} %get-tuple-element.156, s32[1024]{0:T(1024)S(1)} %pad_clamp_fusion.2), kind=kCustom, calls=%fused_computation.clone.1 | custom fusion | bytes 2097280 | tf_op jit(solution)/shard_map/while/body/jit(_take)/gather | solution.py:18
  338.5 6.5 %gather_fusion = bf16[32,128,128]{2,1,0:T(8,128)(2,1)S(1)} fusion(bf16[128,512,128]{2,0,1:T(8,128)(2,1)} %get-tuple-element.156, s32[1024]{0:T(1024)S(1)} %pad_clamp_fusion.2), kind=kCustom, calls=%fused_computation.clone.1 | custom fusion | bytes 2097280 | tf_op jit(solution)/shard_map/while/body/jit(_take)/gather | solution.py:18
  348.9 6.5 %gather_fusion = bf16[32,128,128]{2,1,0:T(8,128)(2,1)S(1)} fusion(bf16[128,512,128]{2,0,1:T(8,128)(2,1)} %get-tuple-element.156, s32[1024]{0:T(1024)S(1)} %pad_clamp_fusion.2), kind=kCustom, calls=%fused_computation.clone.1 | custom fusion | bytes 2097280 | tf_op jit(solution)/shard_map/while/body/jit(_take)/gather | solution.py:18
  359.3 6.5 %gather_fusion = bf16[32,128,128]{2,1,0:T(8,128)(2,1)S(1)} fusion(bf16[128,512,128]{2,0,1:T(8,128)(2,1)} %get-tuple-element.156, s32[1024]{0:T(1024)S(1)} %pad_clamp_fusion.2), kind=kCustom, calls=%fused_computation.clone.1 | custom fusion | bytes 2097280 | tf_op jit(solution)/shard_map/while/body/jit(_take)/gather | solution.py:18
  369.7 6.5 %gather_fusion = bf16[32,128,128]{2,1,0:T(8,128)(2,1)S(1)} fusion(bf16[128,512,128]{2,0,1:T(8,128)(2,1)} %get-tuple-element.156, s32[1024]{0:T(1024)S(1)} %pad_clamp_fusion.2), kind=kCustom, calls=%fused_computation.clone.1 | custom fusion | bytes 2097280 | tf_op jit(solution)/shard_map/while/body/jit(_take)/gather | solution.py:18
  380.1 6.5 %gather_fusion = bf16[32,128,128]{2,1,0:T(8,128)(2,1)S(1)} fusion(bf16[128,512,128]{2,0,1:T(8,128)(2,1)} %get-tuple-element.156, s32[1024]{0:T(1024)S(1)} %pad_clamp_fusion.2), kind=kCustom, calls=%fused_computation.clone.1 | custom fusion | bytes 2097280 | tf_op jit(solution)/shard_map/while/body/jit(_take)/gather | solution.py:18
  390.5 6.5 %gather_fusion = bf16[32,128,128]{2,1,0:T(8,128)(2,1)S(1)} fusion(bf16[128,512,128]{2,0,1:T(8,128)(2,1)} %get-tuple-element.156, s32[1024]{0:T(1024)S(1)} %pad_clamp_fusion.2), kind=kCustom, calls=%fused_computation.clone.1 | custom fusion | bytes 2097280 | tf_op jit(solution)/shard_map/while/body/jit(_take)/gather | solution.py:18
  401.0 6.5 %gather_fusion = bf16[32,128,128]{2,1,0:T(8,128)(2,1)S(1)} fusion(bf16[128,512,128]{2,0,1:T(8,128)(2,1)} %get-tuple-element.156, s32[1024]{0:T(1024)S(1)} %pad_clamp_fusion.2), kind=kCustom, calls=%fused_computation.clone.1 | custom fusion | bytes 2097280 | tf_op jit(solution)/shard_map/while/body/jit(_take)/gather | solution.py:18
  411.4 6.5 %gather_fusion = bf16[32,128,128]{2,1,0:T(8,128)(2,1)S(1)} fusion(bf16[128,512,128]{2,0,1:T(8,128)(2,1)} %get-tuple-element.156, s32[1024]{0:T(1024)S(1)} %pad_clamp_fusion.2), kind=kCustom, calls=%fused_computation.clone.1 | custom fusion | bytes 2097280 | tf_op jit(solution)/shard_map/while/body/jit(_take)/gather | solution.py:18
  421.8 6.5 %gather_fusion = bf16[32,128,128]{2,1,0:T(8,128)(2,1)S(1)} fusion(bf16[128,512,128]{2,0,1:T(8,128)(2,1)} %get-tuple-element.156, s32[1024]{0:T(1024)S(1)} %pad_clamp_fusion.2), kind=kCustom, calls=%fused_computation.clone.1 | custom fusion | bytes 2097280 | tf_op jit(solution)/shard_map/while/body/jit(_take)/gather | solution.py:18
  433.5 10.5 %psum.21 = f32[4096]{0:T(1024)S(1)} all-reduce(f32[4096]{0:T(1024)S(1)} %bitcast.38), channel_id=1, replica_groups=mesh['dp'=8,'walk'=4] {'walk'}, use_global_device_ids=true, to_apply=%region_4.5 | all-reduce | flops 4096 | bytes 32768 | tf_op jit(solution)/shard_map/psum | solution.py:33
  444.0 4.5 fusion.10
  448.5 33.1 %all-gather.6.cloned.1.call-done = bf16[512,4096]{0,1:T(8,128)(2,1)} async-done(((bf16[128,4096]{0,1:T(8,128)(2,1)}), bf16[512,4096]{0,1:T(8,128)(2,1)}) %all-gather.6.cloned.1.call-update) | async-done | bytes 4194320 | tf_op jit(solution)/shard_map/all_gather | solution.py:39
  481.6 3.6 fusion.14
  485.8 70.1 %all-reduce.2.cloned.1.call-done = f32[128,512]{1,0:T(8,128)} async-done(((f32[128,512]{1,0:T(8,128)}), f32[128,512]{1,0:T(8,128)}) %all-reduce.2.cloned.1.call-update) | async-done | bytes 262160 | tf_op jit(solution)/shard_map/psum | solution.py:43
  557.6 6.3 psum.23
  564.5 51.7 %all-gather.8.cloned.1.call-done = bf16[512,8192]{0,1:T(8,128)(2,1)} async-done(((bf16[128,8192]{0,1:T(8,128)(2,1)}), bf16[512,8192]{0,1:T(8,128)(2,1)}) %all-gather.8.cloned.1.call-update) | async-done | bytes 8388624 | tf_op jit(solution)/shard_map/all_gather | solution.py:49
  616.2 9.5 %convolution_subtract_fusion = f32[128,8192]{1,0:T(8,128)} fusion(f32[128,8192]{1,0:T(8,128)} %param.8, bf16[512,8192]{0,1:T(8,128)(2,1)} %all-gather.8.cloned.1.call-done, f32[128,512]{1,0:T(8,128)} %all-reduce.2.cloned.1.call-done, f32[]{:T(128)S(6)} %mul.25), kind=kOutput, calls=%fused_computation.14 | convolution fusion | flops 1074987008 | bytes 17039364 | tf_op jit(solution)/shard_map/dot_general | solution.py:47
  (80 shorter events, 47.0 us)
Async XLA Ops:
  6.5 4.7 copy-start.2
  6.5 235.1 %all-gather.4.cloned.1.call-start = ((), (), s32[]{:S(2)}) async-start(), calls=%async_computation | async-start | bytes 18874368 | tf_op jit(solution)/shard_map/all_gather | solution.py:31
  11.2 470.4 %all-gather.6.cloned.1.call-start = ((), (), s32[]{:S(2)}) async-start(), calls=%async_computation.1 | async-start | bytes 5242880 | tf_op jit(solution)/shard_map/all_gather | solution.py:39
  431.5 12.5 %copy-start = (f32[4096]{0:T(1024)S(1)}, f32[4096]{0:T(1024)}, u32[]{:S(2)}) copy-start(f32[4096]{0:T(1024)} %param.12) | copy-start | bytes 49156
  431.5 12.5 %copy-start.1 = (f32[4096]{0:T(1024)S(1)}, f32[4096]{0:T(1024)}, u32[]{:S(2)}) copy-start(f32[4096]{0:T(1024)} %param.13) | copy-start | bytes 49156
  448.5 107.5 %all-reduce.2.cloned.1.call-start = ((), (), s32[]{:S(2)}) async-start(), calls=%async_computation.2 | async-start | bytes 524288 | tf_op jit(solution)/shard_map/psum | solution.py:43
  485.3 130.9 %all-gather.8.cloned.1.call-start = ((), (), s32[]{:S(2)}) async-start(), calls=%async_computation.3 | async-start | bytes 10485760 | tf_op jit(solution)/shard_map/all_gather | solution.py:49
Sparse Core Ops, SparseCore 0:
  11.3 230.2 all-gather.3
  448.6 32.9 all-gather.5
  485.4 70.5 all-reduce.1
  557.5 58.6 all-gather.7
where the time goes:
time: 635 us; the launch traced here: 632 us
  waiting for transfers between devices  385 us (61%)
  local copies, waits for them, and re-layouts  133 us (21%)
  matrix products  53.6 us (8%)
  other arithmetic  18.3 us (3%)
  blocking collectives  16.7 us (3%)
  between operations  13.8 us (2%)
  loops' own time  11 us (2%)
    all_gather x1, waiting for transfers between devices, local(): gathered = lax.all_gather(field_bf, 'dp', axis=1, tiled=True)  230 us
    gather x16, local copies, waits for them, and re-layouts, one_slot(): blocks = jnp.take(cell_blocks, columns, axis=1)  104 us
    psum x1, waiting for transfers between devices, local(): coupling_mine = lax.psum(partial_rows, 'dp') / WALKERS  70.1 us
    all_gather x1, waiting for transfers between devices, local(): lax.all_gather(field_bf, 'walk', axis=0, tiled=True)  51.7 us
    dot_general x16, matrix products, one_slot(): jnp.einsum('brc,wbc->wbr', sensitive, blocks, preferred_element_type=jnp....  40.4 us
    all_gather x1, waiting for transfers between devices, local(): lax.all_gather(deviation, 'walk', axis=0, tiled=True)  33.1 us
    while x2, local copies, waits for them, and re-layouts, forward(): totals = lax.fori_loop(0, most_live, one_slot, start_sum)  24.3 us
  transfers between devices with their start and end apart: 4, of which 4 were waited for; matrix products, arithmetic and copies ran while one was open for 0% of the time, Pallas kernels for 0%

commit v1 on v0

v1 whole, which is shorter than its diff:
```python
import functools

import jax
import jax.numpy as jnp
from jax import lax
from jax.experimental import pallas as pl
from jax.experimental.pallas import tpu as pltpu
from jax.sharding import PartitionSpec as P

WALKERS = 512
SUB = 2
GROUP = 4


def ring_dp(pos, ring, high):
    pos = lax.rem(pos + 2 * ring, ring)
    col = pos // high
    row = lax.rem(pos, high)
    row = row + lax.rem(col, 2) * (high - 1 - 2 * row)
    return row * (ring // high) + col


def gather_kernel(ring, high, walks, own_ref, all_ref, walk_ref, local_sem, send_sem, recv_sem, walk_send, walk_recv):
    me = lax.axis_index("dp")
    my_walk = lax.axis_index("walk")
    width = ring // high
    row, col = me // width, lax.rem(me, width)
    pos = col * high + row + lax.rem(col, 2) * (high - 1 - 2 * row)
    nxt, prv = ring_dp(pos + 1, ring, high), ring_dp(pos - 1, ring, high)

    barrier = pltpu.get_barrier_semaphore()
    for other in (nxt, prv):
        pl.semaphore_signal(barrier, inc=1, device_id=(other, my_walk), device_id_type=pl.DeviceIdType.MESH)
    for off in range(1, walks):
        pl.semaphore_signal(barrier, inc=1, device_id=(me, lax.rem(my_walk + off, walks)), device_id_type=pl.DeviceIdType.MESH)
    pl.semaphore_wait(barrier, 2 + walks - 1)

    walkers = own_ref.shape[0]
    part = walkers // (2 * SUB)

    def rows(way, sub):
        return pl.ds((way * SUB + sub) * part, part)

    def hop(way, step, sub):
        owner = ring_dp(pos - step if way == 0 else pos + step, ring, high)
        src = own_ref.at[rows(way, sub)] if step == 0 else all_ref.at[owner, rows(way, sub)]
        return pltpu.make_async_remote_copy(
            src_ref=src,
            dst_ref=all_ref.at[owner, rows(way, sub)],
            send_sem=send_sem.at[way, step, sub],
            recv_sem=recv_sem.at[way, step, sub],
            device_id=(nxt if way == 0 else prv, my_walk),
            device_id_type=pl.DeviceIdType.MESH,
        )

    hops = {}
    for sub in range(SUB):
        for way in range(2):
            hops[way, 0, sub] = hop(way, 0, sub)
            hops[way, 0, sub].start()
    mine = pltpu.make_async_copy(own_ref, all_ref.at[me], local_sem.at[0])
    mine.start()
    mine_walk = pltpu.make_async_copy(own_ref, walk_ref.at[my_walk], local_sem.at[1])
    mine_walk.start()
    sent = []
    for off in range(1, walks):
        copy = pltpu.make_async_remote_copy(
            src_ref=own_ref,
            dst_ref=walk_ref.at[my_walk],
            send_sem=walk_send.at[off - 1],
            recv_sem=walk_recv.at[off - 1],
            device_id=(me, lax.rem(my_walk + off, walks)),
            device_id_type=pl.DeviceIdType.MESH,
        )
        copy.start()
        sent.append(copy)
    for step in range(1, ring - 1):
        for sub in range(SUB):
            for way in range(2):
                hops[way, step - 1, sub].wait_recv()
                hops[way, step, sub] = hop(way, step, sub)
                hops[way, step, sub].start()
    for sub in range(SUB):
        for way in range(2):
            hops[way, ring - 2, sub].wait_recv()
    for copy in hops.values():
        copy.wait_send()
    for copy in sent:
        copy.wait()
    mine.wait()
    mine_walk.wait()


def gather(field_bf, ring, walks):
    high = 4
    walkers, cells = field_bf.shape
    return pl.pallas_call(
        functools.partial(gather_kernel, ring, high, walks),
        out_shape=(
            jax.ShapeDtypeStruct((ring, walkers, cells), jnp.bfloat16),
            jax.ShapeDtypeStruct((walks, walkers, cells), jnp.bfloat16),
        ),
        in_specs=[pl.BlockSpec(memory_space=pl.ANY)],
        out_specs=(pl.BlockSpec(memory_space=pl.ANY), pl.BlockSpec(memory_space=pl.ANY)),
        scratch_shapes=[
            pltpu.SemaphoreType.DMA((2,)),
            pltpu.SemaphoreType.DMA((2, ring - 1, SUB)),
            pltpu.SemaphoreType.DMA((2, ring - 1, SUB)),
            pltpu.SemaphoreType.DMA((walks - 1,)),
            pltpu.SemaphoreType.DMA((walks - 1,)),
        ],
        compiler_params=pltpu.CompilerParams(collective_id=0, has_side_effects=True),
        name="gather_fields",
    )(field_bf)


def forward_kernel(per_dev, slots, index_ref, count_ref, all_ref, sens_ref, pred_ref, sum_ref, held, lhs, load_sem):
    blk = pl.program_id(0)
    tile = sens_ref.shape[-1]
    ring = held.shape[0]

    @pl.when(blk == 0)
    def _():
        copies = [pltpu.make_async_copy(all_ref.at[d], held.at[d], load_sem.at[d]) for d in range(ring)]
        for copy in copies:
            copy.start()
        for copy in copies:
            copy.wait()

    count = count_ref[blk]
    pred_ref[...] = jnp.zeros_like(pred_ref)

    def group(g, carry):
        for k in range(GROUP):
            slot = g * GROUP + k
            block = index_ref[blk, slot]
            start = pl.multiple_of(lax.rem(block, per_dev) * tile, tile)
            piece = held[block // per_dev, :, pl.ds(start, tile)]
            lhs[:, k * tile : (k + 1) * tile] = jnp.where(slot < count, piece, jnp.zeros_like(piece))
        total = pred_ref[...]
        for k in range(0, GROUP, 2):
            right = jnp.concatenate([sens_ref[0, g * GROUP + k], sens_ref[0, g * GROUP + k + 1]], axis=1)
            total += lax.dot_general(
                lhs[:, k * tile : (k + 2) * tile], right, (((1,), (1,)), ((), ())), preferred_element_type=jnp.float32
            )
        pred_ref[...] = total
        return carry

    lax.fori_loop(0, (count + GROUP - 1) // GROUP, group, 0)
    sum_ref[...] = jnp.sum(pred_ref[...], axis=0, keepdims=True)


def forward(gathered, sensitivity, tile_index, tile_count):
    ring, walkers, cells = gathered.shape
    nblocks, slots, tile, _ = sensitivity.shape
    return pl.pallas_call(
        functools.partial(forward_kernel, cells // tile, slots),
        out_shape=(
            jax.ShapeDtypeStruct((walkers, nblocks * tile), jnp.float32),
            jax.ShapeDtypeStruct((1, nblocks * tile), jnp.float32),
        ),
        grid_spec=pltpu.PrefetchScalarGridSpec(
            num_scalar_prefetch=2,
            grid=(nblocks,),
            in_specs=[
                pl.BlockSpec(memory_space=pl.ANY),
                pl.BlockSpec((1, slots, tile, tile), lambda b, *_: (b, 0, 0, 0)),
            ],
            out_specs=(
                pl.BlockSpec((walkers, tile), lambda b, *_: (0, b)),
                pl.BlockSpec((1, tile), lambda b, *_: (0, b)),
            ),
            scratch_shapes=[
                pltpu.VMEM((ring, walkers, cells), jnp.bfloat16),
                pltpu.VMEM((walkers, GROUP * tile), jnp.bfloat16),
                pltpu.SemaphoreType.DMA((ring,)),
            ],
        ),
        compiler_params=pltpu.CompilerParams(vmem_limit_bytes=56 * 2**20),
        name="forward_rays",
    )(tile_index, tile_count, gathered, sensitivity)


def local(ring, walks, fields, sensitivity, tile_index, tile_count, observed, precision):
    field_bf = fields.astype(jnp.bfloat16)
    gathered, walk_fields = gather(field_bf, ring, walks)
    predicted, pred_part = forward(gathered, sensitivity, tile_index, tile_count)
    pred_mean = lax.psum(pred_part[0], "walk") / WALKERS
    deviation = (predicted - pred_mean[None, :]).astype(jnp.bfloat16)
    misfit = (precision[None, :] * (predicted - observed[None, :])).astype(jnp.bfloat16)
    partial_rows = lax.dot_general(
        misfit,
        lax.all_gather(deviation, "walk", axis=0, tiled=True),
        (((1,), (1,)), ((), ())),
        preferred_element_type=jnp.float32,
    )
    coupling_mine = lax.psum(partial_rows, "dp") / WALKERS
    squares = lax.psum(jnp.sum(coupling_mine * coupling_mine), "walk")
    spread = jnp.sqrt(squares / (WALKERS * WALKERS) + 1e-06)
    weights = (8.0 * coupling_mine / (WALKERS * spread)).astype(jnp.bfloat16)
    update = jnp.dot(weights, walk_fields.reshape(WALKERS, -1), preferred_element_type=jnp.float32)
    return fields - update


def solution(mesh):
    placed = (P("walk", "dp"), P("dp", None, None, None), P("dp", None), P("dp"), P("dp"), P("dp"))
    return jax.shard_map(
        functools.partial(local, mesh.shape["dp"], mesh.shape["walk"]),
        mesh=mesh, in_specs=placed, out_specs=P("walk", "dp"), check_vma=False,
    )
```

time: 635 us -> 359 us (0.57)
  waiting for transfers between devices: 385 us -> 111 us
  Pallas kernels: 0 us -> 194 us
  local copies, waits for them, and re-layouts: 133 us -> 1.38 us
  matrix products: 53.6 us -> 12.4 us
  loops' own time: 11 us -> 0 us
  other arithmetic: 18.3 us -> 8.13 us
    all_gather x2 -> x0, waiting for transfers between devices: 281 us -> none  [the longest x1 230 us: local(): gathered = lax.all_gather(field_bf, 'dp', axis=1, tiled=True)]
    pallas_call x0 -> x2, Pallas kernels: none -> 194 us  [the longest x1 164 us: gather(): pl.pallas_call(functools.partial(gather_kernel, ring, high, walks), out_s...]
    gather x16 -> x0, local copies, waits for them, and re-layouts: 104 us -> none  [one_slot(): blocks = jnp.take(cell_blocks, columns, axis=1)]
    dot_general x17 -> x1, matrix products: 49.9 us -> 7.95 us  [local(): jnp.dot(weights, walk_fields.reshape(WALKERS, -1), preferred_element_type...]
    while x2 -> x0, local copies, waits for them, and re-layouts: 24.3 us -> none  [forward(): totals = lax.fori_loop(0, most_live, one_slot, start_sum)]
    reduce_and x16 -> x0, other arithmetic: 11.2 us -> none  [one_slot(): blocks = jnp.take(cell_blocks, columns, axis=1)]
    another operation x1 -> x0, loops' own time: 11 us -> none  [forward(): totals = lax.fori_loop(0, most_live, one_slot, start_sum)]
    all_gather x1, waiting for transfers between devices: 33.1 us -> 40.4 us  [local(): lax.all_gather(deviation, 'walk', axis=0, tiled=True)]
  transfers between devices with their start and end apart: 4 -> 2, of which waited for: 4 -> 2; matrix products, arithmetic and copies ran while one was open for 0% -> 0% of each run, Pallas kernels for 0% -> 0%
where the time goes in v1:
time: 359 us; the launch traced here: 358 us
  Pallas kernels  194 us (54%)
  waiting for transfers between devices  111 us (31%)
  blocking collectives  17.1 us (5%)
  between operations  14.1 us (4%)
  matrix products  12.4 us (3%)
  other arithmetic  8.13 us (2%)
    pallas_call x1, Pallas kernels, gather(): pl.pallas_call(functools.partial(gather_kernel, ring, high, walks), out_s...  164 us
    psum x1, waiting for transfers between devices, local(): coupling_mine = lax.psum(partial_rows, 'dp') / WALKERS  70.7 us
    all_gather x1, waiting for transfers between devices, local(): lax.all_gather(deviation, 'walk', axis=0, tiled=True)  40.4 us
    pallas_call x1, Pallas kernels, forward(): pl.pallas_call(functools.partial(forward_kernel, cells // tile, slots), o...  30 us
    psum x1, blocking collectives, local(): pred_mean = lax.psum(pred_part[0], 'walk') / WALKERS  10.8 us
    dot_general x1, matrix products, local(): jnp.dot(weights, walk_fields.reshape(WALKERS, -1), preferred_element_type...  7.95 us
  transfers between devices with their start and end apart: 2, of which 2 were waited for; matrix products, arithmetic and copies ran while one was open for 0% of the time, Pallas kernels for 0%

profile of v1, /device:TPU:0, one launch (start us, length us, event | category | flops | bytes accessed | tf_op | source)
XLA Modules:
  0.0 358.0 jit_solution(16580913008089606276)
XLA Ops:
  6.5 0.0 all-gather.2.cloned.1.call-start
  6.5 1.4 copy.7.index_ref
  7.9 3.8 %convert_element_type.12.own_ref = bf16[128,8192]{1,0:T(8,128)(2,1)} convert(f32[128,8192]{1,0:T(8,128)} %param.6) | non-fusion elementwise | flops 1048576 | bytes 6291456 | tf_op jit(solution)/shard_map/convert_element_type | solution.py:185
  11.7 163.8 %gather_fields.1 = (bf16[8,128,8192]{2,1,0:T(8,128)(2,1)}, bf16[4,128,8192]{2,1,0:T(8,128)(2,1)}) custom-call(bf16[128,8192]{1,0:T(8,128)(2,1)} %convert_element_type.12.own_ref), custom_call_target="tpu_custom_call" | custom-call | tf_op jit(solution)/shard_map/gather_fields/pallas_call | solution.py:97
  175.5 30.0 %forward_rays.1 = (f32[128,4096]{1,0:T(8,128)}, f32[1,4096]{1,0:T(1,128)}) custom-call(s32[32,16]{1,0:T(8,128)} %copy.7.index_ref, s32[32]{0:T(128)} %count_ref.1, bf16[8,128,8192]{2,1,0:T(8,128)(2,1)} %get-tuple-element.9.all_ref, bf16[32,16,128,128]{3,2,1,0:T(8,128)(2,1)} %sens_ref.1), custom_call_target="tpu_custom_call" | custom-call | tf_op jit(solution)/shard_map/forward_rays/pallas_call | solution.py:156
  205.4 0.0 copy-start
  205.4 0.0 copy-start.1
  205.4 0.0 copy-start.2
  205.5 10.8 %psum.21 = f32[4096]{0:T(1024)S(1)} all-reduce(f32[4096]{0:T(1024)} %bitcast.5), channel_id=1, replica_groups=mesh['dp'=8,'walk'=4] {'walk'}, use_global_device_ids=true, to_apply=%region_0.0 | all-reduce | flops 4096 | bytes 32768 | tf_op jit(solution)/shard_map/psum | solution.py:188
  216.3 2.7 subtract_convert_fusion
  219.0 0.0 all-gather.2.cloned.1.call-update
  219.0 0.0 all-reduce.2.cloned.1.call-start
  219.1 40.4 %all-gather.2.cloned.1.call-done = bf16[512,4096]{1,0:T(8,128)(2,1)} async-done(((bf16[128,4096]{1,0:T(8,128)(2,1)}), bf16[512,4096]{1,0:T(8,128)(2,1)}) %all-gather.2.cloned.1.call-update) | async-done | bytes 4194320 | tf_op jit(solution)/shard_map/all_gather | solution.py:193
  259.5 0.0 copy-done
  259.5 0.0 copy-done.1
  259.5 0.0 copy-done.2
  259.5 4.4 %fusion = f32[128,512]{1,0:T(8,128)} fusion(bf16[512,4096]{1,0:T(8,128)(2,1)} %all-gather.2.cloned.1.call-done, f32[128,4096]{1,0:T(8,128)S(1)} %copy-done, f32[4096]{0:T(1024)S(1)} %copy-done.1, f32[4096]{0:T(1024)S(1)} %copy-done.2), kind=kOutput, calls=%fused_computation.3 | convolution fusion | flops 538443776 | bytes 6586368 | tf_op jit(solution)/shard_map/dot_general | solution.py:191
  263.9 0.0 all-reduce.2.cloned.1.call-update
  263.9 70.7 %all-reduce.2.cloned.1.call-done = f32[128,512]{1,0:T(8,128)} async-done(((f32[128,512]{1,0:T(8,128)}), f32[128,512]{1,0:T(8,128)}) %all-reduce.2.cloned.1.call-update) | async-done | bytes 262160 | tf_op jit(solution)/shard_map/psum | solution.py:197
  334.6 1.6 multiply_reduce_fusion
  336.2 6.3 %psum.23 = f32[]{:T(128)} all-reduce(f32[]{:T(128)} %multiply_reduce_fusion), channel_id=1, replica_groups=mesh['dp'=8,'walk'=4] {'walk'}, use_global_device_ids=true, to_apply=%region_3.0 | all-reduce | flops 1 | bytes 8 | tf_op jit(solution)/shard_map/psum | solution.py:198
  343.2 8.0 %convolution_subtract_fusion = f32[128,8192]{1,0:T(8,128)} fusion(f32[128,8192]{1,0:T(8,128)} %param.6, bf16[512,8192]{1,0:T(8,128)(2,1)} %bitcast.4, f32[128,512]{1,0:T(8,128)} %all-reduce.2.cloned.1.call-done, f32[]{:T(128)S(6)} %mul.25), kind=kOutput, calls=%fused_computation | convolution fusion | flops 1074987008 | bytes 17039364 | tf_op jit(solution)/shard_map/dot_general | solution.py:201
  (1 shorter events, 0.0 us)
Async XLA Ops:
  6.5 252.9 %all-gather.2.cloned.1.call-start = ((), (), s32[]{:S(2)}) async-start(), calls=%async_computation | async-start | bytes 5242880 | tf_op jit(solution)/shard_map/all_gather | solution.py:193
  205.4 54.1 %copy-start = (f32[128,4096]{1,0:T(8,128)S(1)}, f32[128,4096]{1,0:T(8,128)}, u32[]{:S(2)}) copy-start(f32[128,4096]{1,0:T(8,128)} %get-tuple-element.10) | copy-start | bytes 6291460
  205.4 54.0 %copy-start.1 = (f32[4096]{0:T(1024)S(1)}, f32[4096]{0:T(1024)}, u32[]{:S(2)}) copy-start(f32[4096]{0:T(1024)} %param.10) | copy-start | bytes 49156
  205.4 54.0 %copy-start.2 = (f32[4096]{0:T(1024)S(1)}, f32[4096]{0:T(1024)}, u32[]{:S(2)}) copy-start(f32[4096]{0:T(1024)} %param.11) | copy-start | bytes 49156
  219.0 115.6 %all-reduce.2.cloned.1.call-start = ((), (), s32[]{:S(2)}) async-start(), calls=%async_computation.1 | async-start | bytes 524288 | tf_op jit(solution)/shard_map/psum | solution.py:197
Sparse Core Ops, SparseCore 0:
  219.2 40.2 all-gather.1
  264.0 70.5 all-reduce.1

commit v2 on v1

--- a/solution.py
+++ b/solution.py
@@ -9,7 +9,8 @@
 
 WALKERS = 512
 SUB = 2
-GROUP = 4
+GROUP = 8
+CHUNKS = 4
 
 
 def ring_dp(pos, ring, high):
@@ -114,7 +115,7 @@
     )(field_bf)
 
 
-def forward_kernel(per_dev, slots, index_ref, count_ref, all_ref, sens_ref, pred_ref, sum_ref, held, lhs, load_sem):
+def forward_kernel(per_dev, slots, index_ref, count_ref, all_ref, sens_ref, pred_ref, sum_ref, held, load_sem):
     blk = pl.program_id(0)
     tile = sens_ref.shape[-1]
     ring = held.shape[0]
@@ -131,19 +132,18 @@
     pred_ref[...] = jnp.zeros_like(pred_ref)
 
     def group(g, carry):
+        left, right = [], []
         for k in range(GROUP):
             slot = g * GROUP + k
             block = index_ref[blk, slot]
             start = pl.multiple_of(lax.rem(block, per_dev) * tile, tile)
             piece = held[block // per_dev, :, pl.ds(start, tile)]
-            lhs[:, k * tile : (k + 1) * tile] = jnp.where(slot < count, piece, jnp.zeros_like(piece))
-        total = pred_ref[...]
-        for k in range(0, GROUP, 2):
-            right = jnp.concatenate([sens_ref[0, g * GROUP + k], sens_ref[0, g * GROUP + k + 1]], axis=1)
-            total += lax.dot_general(
-                lhs[:, k * tile : (k + 2) * tile], right, (((1,), (1,)), ((), ())), preferred_element_type=jnp.float32
-            )
-        pred_ref[...] = total
+            left.append(jnp.where(slot < count, piece, jnp.zeros_like(piece)))
+            right.append(sens_ref[0, slot])
+        pred_ref[...] += lax.dot_general(
+            jnp.concatenate(left, axis=1), jnp.concatenate(right, axis=1),
+            (((1,), (1,)), ((), ())), preferred_element_type=jnp.float32,
+        )
         return carry
 
     lax.fori_loop(0, (count + GROUP - 1) // GROUP, group, 0)
@@ -172,7 +172,6 @@
             ),
             scratch_shapes=[
                 pltpu.VMEM((ring, walkers, cells), jnp.bfloat16),
-                pltpu.VMEM((walkers, GROUP * tile), jnp.bfloat16),
                 pltpu.SemaphoreType.DMA((ring,)),
             ],
         ),
@@ -181,23 +180,151 @@
     )(tile_index, tile_count, gathered, sensitivity)
 
 
+def tail_kernel(
+    ring, walks, pred_ref, sum_ref, obs_ref, prec_ref, out_ref, sums, mis, devs, acc, part, parts_in, coup, sq_own, sq_in,
+    sum_send, sum_recv, sib_send, sib_recv, far_send, far_recv, relay_send, relay_recv,
+    part_send, part_recv, coup_send, coup_recv, sq_send, sq_recv,
+):
+    me = lax.axis_index("dp")
+    my_walk = lax.axis_index("walk")
+    far = walks // 2
+    my_far, core = my_walk // 2, lax.rem(my_walk, 2)
+    sibling = my_far * 2 + 1 - core
+    walkers = pred_ref.shape[0]
+    width = mis.shape[2]
+    piece = walkers // ring
+
+    def send(src, dst, send_sem, recv_sem, dp, walk):
+        copy = pltpu.make_async_remote_copy(
+            src_ref=src, dst_ref=dst, send_sem=send_sem, recv_sem=recv_sem,
+            device_id=(dp, walk), device_id_type=pl.DeviceIdType.MESH,
+        )
+        copy.start()
+        return copy
+
+    barrier = pltpu.get_barrier_semaphore()
+    for off in range(1, walks):
+        pl.semaphore_signal(barrier, inc=1, device_id=(me, lax.rem(my_walk + off, walks)), device_id_type=pl.DeviceIdType.MESH)
+    for off in range(1, ring):
+        pl.semaphore_signal(barrier, inc=1, device_id=(lax.rem(me + off, ring), my_walk), device_id_type=pl.DeviceIdType.MESH)
+    pl.semaphore_wait(barrier, walks + ring - 2)
+
+    sent_sums = [
+        send(sum_ref, sums.at[off - 1], sum_send.at[off - 1], sum_recv.at[off - 1], me, lax.rem(my_walk + off, walks))
+        for off in range(1, walks)
+    ]
+    for n in range(CHUNKS):
+        cols = slice(n * width, (n + 1) * width)
+        mis[n] = (prec_ref[:, cols] * (pred_ref[:, cols] - obs_ref[:, cols])).astype(jnp.bfloat16)
+    for copy in sent_sums:
+        copy.wait_recv()
+
+    to_sibling, to_far, relays = [], {}, {}
+    for n in range(CHUNKS):
+        cols = slice(n * width, (n + 1) * width)
+        total = sum_ref[:, cols]
+        for off in range(1, walks):
+            total = total + sums[off - 1, :, cols]
+        mean = total / WALKERS
+        devs[n, my_walk] = (pred_ref[:, cols] - mean).astype(jnp.bfloat16)
+        block = devs.at[n, my_walk]
+        for off in range(1, far):
+            other = lax.rem(my_far + off, far) * 2 + core
+            to_far[n, off] = send(block, block, far_send.at[off - 1, n], far_recv.at[off - 1, n], me, other)
+        to_sibling.append(send(block, block, sib_send.at[n], sib_recv.at[n], me, sibling))
+
+    def couple(n):
+        to_sibling[n].wait_recv()
+        for off in range(1, far):
+            relays[n, off].wait_recv()
+        every = devs[n].reshape(walks * walkers, width)
+        product = lax.dot_general(mis[n], every, (((1,), (1,)), ((), ())), preferred_element_type=jnp.float32)
+        acc[...] = product if n == 0 else acc[...] + product
+
+    for n in range(CHUNKS):
+        for off in range(1, far):
+            to_far[n, off].wait_recv()
+            origin = lax.rem(my_far + far - off, far) * 2 + core
+            block = devs.at[n, origin]
+            relays[n, off] = send(block, block, relay_send.at[off - 1, n], relay_recv.at[off - 1, n], me, sibling)
+        if n > 0:
+            couple(n - 1)
+    couple(CHUNKS - 1)
+
+    for d in range(ring):
+        part[d] = acc[d * piece : (d + 1) * piece, :]
+    sent_parts = []
+    for off in range(1, ring):
+        other = lax.rem(me + off, ring)
+        sent_parts.append(
+            send(part.at[other], parts_in.at[off - 1], part_send.at[off - 1], part_recv.at[off - 1], other, my_walk)
+        )
+    whole = part[me]
+    for off in range(1, ring):
+        sent_parts[off - 1].wait_recv()
+        whole = whole + parts_in[off - 1]
+    coup[me] = whole / WALKERS
+    sent_coup = [
+        send(coup.at[me], coup.at[me], coup_send.at[off - 1], coup_recv.at[off - 1], lax.rem(me + off, ring), my_walk)
+        for off in range(1, ring)
+    ]
+    for copy in sent_coup:
+        copy.wait_recv()
+    coupling = jnp.concatenate([coup[d] for d in range(ring)], axis=0)
+    sq_own[...] = jnp.sum(coupling * coupling, axis=0, keepdims=True)
+    sent_sq = [
+        send(sq_own, sq_in.at[off - 1], sq_send.at[off - 1], sq_recv.at[off - 1], me, lax.rem(my_walk + off, walks))
+        for off in range(1, walks)
+    ]
+    squares = sq_own[...]
+    for off in range(1, walks):
+        sent_sq[off - 1].wait_recv()
+        squares = squares + sq_in[off - 1]
+    spread = jnp.sqrt(jnp.sum(squares, axis=1, keepdims=True) / (WALKERS * WALKERS) + 1e-06)
+    out_ref[...] = (8.0 * coupling / (WALKERS * spread)).astype(jnp.bfloat16)
+    for copy in sent_sums + to_sibling + list(to_far.values()) + list(relays.values()) + sent_parts + sent_coup + sent_sq:
+        copy.wait_send()
+
+
+def tail(predicted, pred_part, observed, precision, ring, walks):
+    walkers, rows = predicted.shape
+    width = rows // CHUNKS
+    piece = walkers // ring
+    dma = pltpu.SemaphoreType.DMA
+    far = walks // 2
+    return pl.pallas_call(
+        functools.partial(tail_kernel, ring, walks),
+        out_shape=jax.ShapeDtypeStruct((walkers, WALKERS), jnp.bfloat16),
+        in_specs=[pl.BlockSpec(memory_space=pltpu.VMEM)] * 4,
+        out_specs=pl.BlockSpec(memory_space=pltpu.VMEM),
+        scratch_shapes=[
+            pltpu.VMEM((walks - 1, 1, rows), jnp.float32),
+            pltpu.VMEM((CHUNKS, walkers, width), jnp.bfloat16),
+            pltpu.VMEM((CHUNKS, walks, walkers, width), jnp.bfloat16),
+            pltpu.VMEM((walkers, WALKERS), jnp.float32),
+            pltpu.VMEM((ring, piece, WALKERS), jnp.float32),
+            pltpu.VMEM((ring - 1, piece, WALKERS), jnp.float32),
+            pltpu.VMEM((ring, piece, WALKERS), jnp.float32),
+            pltpu.VMEM((1, WALKERS), jnp.float32),
+            pltpu.VMEM((walks - 1, 1, WALKERS), jnp.float32),
+            dma((walks - 1,)), dma((walks - 1,)),
+            dma((CHUNKS,)), dma((CHUNKS,)),
+            dma((far - 1, CHUNKS)), dma((far - 1, CHUNKS)),
+            dma((far - 1, CHUNKS)), dma((far - 1, CHUNKS)),
+            dma((ring - 1,)), dma((ring - 1,)),
+            dma((ring - 1,)), dma((ring - 1,)),
+            dma((walks - 1,)), dma((walks - 1,)),
+        ],
+        compiler_params=pltpu.CompilerParams(collective_id=1, has_side_effects=True, vmem_limit_bytes=40 * 2**20),
+        name="couple_walkers",
+    )(predicted, pred_part, observed[None], precision[None])
+
+
 def local(ring, walks, fields, sensitivity, tile_index, tile_count, observed, precision):
     field_bf = fields.astype(jnp.bfloat16)
     gathered, walk_fields = gather(field_bf, ring, walks)
     predicted, pred_part = forward(gathered, sensitivity, tile_index, tile_count)
-    pred_mean = lax.psum(pred_part[0], "walk") / WALKERS
-    deviation = (predicted - pred_mean[None, :]).astype(jnp.bfloat16)
-    misfit = (precision[None, :] * (predicted - observed[None, :])).astype(jnp.bfloat16)
-    partial_rows = lax.dot_general(
-        misfit,
-        lax.all_gather(deviation, "walk", axis=0, tiled=True),
-        (((1,), (1,)), ((), ())),
-        preferred_element_type=jnp.float32,
-    )
-    coupling_mine = lax.psum(partial_rows, "dp") / WALKERS
-    squares = lax.psum(jnp.sum(coupling_mine * coupling_mine), "walk")
-    spread = jnp.sqrt(squares / (WALKERS * WALKERS) + 1e-06)
-    weights = (8.0 * coupling_mine / (WALKERS * spread)).astype(jnp.bfloat16)
+    weights = tail(predicted, pred_part, observed, precision, ring, walks)
     update = jnp.dot(weights, walk_fields.reshape(WALKERS, -1), preferred_element_type=jnp.float32)
     return fields - update
 

time: 359 us -> 260 us (0.72)
  waiting for transfers between devices: 111 us -> 0 us
  Pallas kernels: 194 us -> 244 us
  blocking collectives: 17.1 us -> 0 us
  between operations: 14.1 us -> 0.08 us
  matrix products: 12.4 us -> 6.68 us
  other arithmetic: 8.13 us -> 3.76 us
    psum x1 -> x0, waiting for transfers between devices: 70.7 us -> none  [local(): coupling_mine = lax.psum(partial_rows, 'dp') / WALKERS]
    pallas_call x0 -> x1, Pallas kernels: none -> 50.2 us  [tail(): pl.pallas_call(functools.partial(tail_kernel, ring, walks), out_shape=jax...]
    all_gather x1 -> x0, waiting for transfers between devices: 40.4 us -> none  [local(): lax.all_gather(deviation, 'walk', axis=0, tiled=True)]
    psum x2 -> x0, blocking collectives: 17.1 us -> none  [the longest x1 10.8 us: local(): pred_mean = lax.psum(pred_part[0], 'walk') / WALKERS]
    dot_general x1 -> x0, matrix products: 4.41 us -> none  [local(): lax.dot_general(misfit, lax.all_gather(deviation, 'walk', axis=0, tiled=T...]
  transfers between devices with their start and end apart: 2 -> 0, of which waited for: 2 -> 0; matrix products, arithmetic and copies ran while one was open for 0% -> 0% of each run, Pallas kernels for 0% -> 0%
where the time goes in v2:
time: 260 us; the launch traced here: 259 us
  Pallas kernels  244 us (94%)
  matrix products  6.68 us (3%)
  other arithmetic  3.76 us (1%)
  local copies, waits for them, and re-layouts  3.69 us (1%)
    pallas_call x1, Pallas kernels, gather(): pl.pallas_call(functools.partial(gather_kernel, ring, high, walks), out_s...  164 us
    pallas_call x1, Pallas kernels, tail(): pl.pallas_call(functools.partial(tail_kernel, ring, walks), out_shape=jax...  50.2 us
    pallas_call x1, Pallas kernels, forward(): pl.pallas_call(functools.partial(forward_kernel, cells // tile, slots), o...  30.5 us
    dot_general x1, matrix products, local(): jnp.dot(weights, walk_fields.reshape(WALKERS, -1), preferred_element_type...  6.68 us

profile of v2, /device:TPU:0, one launch (start us, length us, event | category | flops | bytes accessed | tf_op | source)
XLA Modules:
  0.0 258.7 jit_solution(17635117045361282966)
XLA Ops:
  0.0 1.4 copy.7.index_ref
  1.4 3.8 %convert_element_type.3.own_ref = bf16[128,8192]{1,0:T(8,128)(2,1)} convert(f32[128,8192]{1,0:T(8,128)} %param.6) | non-fusion elementwise | flops 1048576 | bytes 6291456 | tf_op jit(solution)/shard_map/convert_element_type | solution.py:324
  5.1 163.8 %gather_fields.1 = (bf16[8,128,8192]{2,1,0:T(8,128)(2,1)}, bf16[4,128,8192]{2,1,0:T(8,128)(2,1)}) custom-call(bf16[128,8192]{1,0:T(8,128)(2,1)} %convert_element_type.3.own_ref), custom_call_target="tpu_custom_call" | custom-call | tf_op jit(solution)/shard_map/gather_fields/pallas_call | solution.py:98
  168.9 0.0 copy-start.1
  168.9 0.0 copy-start.2
  168.9 0.0 copy-start.4
  169.0 30.5 %forward_rays.1 = (f32[128,4096]{1,0:T(8,128)}, f32[1,4096]{1,0:T(1,128)}) custom-call(s32[32,16]{1,0:T(8,128)} %copy.7.index_ref, s32[32]{0:T(128)} %count_ref.1, bf16[8,128,8192]{2,1,0:T(8,128)(2,1)} %get-tuple-element.9.all_ref, bf16[32,16,128,128]{3,2,1,0:T(8,128)(2,1)} %sens_ref.1), custom_call_target="tpu_custom_call" | custom-call | tf_op jit(solution)/shard_map/forward_rays/pallas_call | solution.py:156
  199.5 0.0 copy-done.1
  199.5 0.0 copy-done.2
  199.5 0.0 copy-start
  199.5 1.6 copy-done
  201.1 0.0 copy-start.3
  201.1 0.7 copy-done.3
  201.8 50.2 %couple_walkers.1 = bf16[128,512]{1,0:T(8,128)(2,1)S(1)} custom-call(f32[128,4096]{1,0:T(8,128)S(1)} %copy-done, f32[1,4096]{1,0:T(1,128)S(1)} %copy-done.3, f32[1,4096]{1,0:T(1,128)S(1)} %bitcast.5, f32[1,4096]{1,0:T(1,128)S(1)} %bitcast.6), custom_call_target="tpu_custom_call" | custom-call | tf_op jit(solution)/shard_map/couple_walkers/pallas_call | solution.py:295
  252.0 0.0 copy-done.4
  252.0 6.7 %convolution_subtract_fusion = f32[128,8192]{1,0:T(8,128)} fusion(f32[128,8192]{1,0:T(8,128)S(1)} %copy-done.4, bf16[128,512]{1,0:T(8,128)(2,1)S(1)} %couple_walkers.1, bf16[512,8192]{1,0:T(8,128)(2,1)} %bitcast.7), kind=kOutput, calls=%fused_computation | convolution fusion | flops 1074790400 | bytes 16908288 | tf_op jit(solution)/shard_map/dot_general | solution.py:328
Async XLA Ops:
  168.9 30.6 %copy-start.1 = (f32[4096]{0:T(1024)S(1)}, f32[4096]{0:T(1024)}, u32[]{:S(2)}) copy-start(f32[4096]{0:T(1024)} %param.10) | copy-start | bytes 49156
  168.9 30.6 %copy-start.2 = (f32[4096]{0:T(1024)S(1)}, f32[4096]{0:T(1024)}, u32[]{:S(2)}) copy-start(f32[4096]{0:T(1024)} %param.11) | copy-start | bytes 49156
  168.9 83.0 %copy-start.4 = (f32[128,8192]{1,0:T(8,128)S(1)}, f32[128,8192]{1,0:T(8,128)}, u32[]{:S(2)}) copy-start(f32[128,8192]{1,0:T(8,128)} %param.6) | copy-start | bytes 12582916
  199.5 1.6 copy-start
  201.1 0.7 copy-start.3

commit v3 on v0

v3 whole, which is shorter than its diff:
```python
import functools

import jax
import jax.numpy as jnp
from jax import lax
from jax.experimental import pallas as pl
from jax.experimental.pallas import tpu as pltpu
from jax.sharding import PartitionSpec as P

WALKERS = 512
SUB = 2
CHUNKS = 4
HIGH = 4


def ring_dp(pos, ring, high):
    pos = lax.rem(pos + 2 * ring, ring)
    col = pos // high
    row = lax.rem(pos, high)
    row = row + lax.rem(col, 2) * (high - 1 - 2 * row)
    return row * (ring // high) + col


def step_kernel(
    ring, high, walks, index_ref, fields_ref, sens_ref, obs_ref, prec_ref, out_ref, walk_ref,
    wide, own, held, sens, pred, own_sums, sums, mis, devs, acc, part, parts_in, coup, sq_own, sq_in,
    wide_sem, sens_sem, local_sem, ring_send, ring_recv, walk_send, walk_recv,
    sum_send, sum_recv, sib_send, sib_recv, far_send, far_recv, relay_send, relay_recv,
    part_send, part_recv, coup_send, coup_recv, sq_send, sq_recv,
):
    me = lax.axis_index("dp")
    my_walk = lax.axis_index("walk")
    grid_width = ring // high
    row, col = me // grid_width, lax.rem(me, grid_width)
    pos = col * high + row + lax.rem(col, 2) * (high - 1 - 2 * row)
    nxt, prv = ring_dp(pos + 1, ring, high), ring_dp(pos - 1, ring, high)
    far = walks // 2
    my_far, core = my_walk // 2, lax.rem(my_walk, 2)
    sibling = my_far * 2 + 1 - core
    walkers = wide.shape[0]
    nblocks, slots, tile = sens.shape[0], sens.shape[1], sens.shape[2]
    per_dev = wide.shape[1] // tile
    width = mis.shape[2]
    piece = walkers // ring
    span = per_dev // (2 * SUB)
    batch = nblocks // CHUNKS

    def send(src, dst, send_sem, recv_sem, dp, walk):
        copy = pltpu.make_async_remote_copy(
            src_ref=src, dst_ref=dst, send_sem=send_sem, recv_sem=recv_sem,
            device_id=(dp, walk), device_id_type=pl.DeviceIdType.MESH,
        )
        copy.start()
        return copy

    order = [(way, sub) for sub in range(SUB) for way in range(2)]

    def share(way, sub):
        first = (way * SUB + sub) * span
        return slice(first * tile, (first + span) * tile)

    loads = {}
    for i, key in enumerate(order):
        loads[key] = pltpu.make_async_copy(fields_ref.at[:, share(*key)], wide.at[:, share(*key)], wide_sem.at[i])
        loads[key].start()

    barrier = pltpu.get_barrier_semaphore()
    for off in range(1, walks):
        pl.semaphore_signal(barrier, inc=1, device_id=(me, lax.rem(my_walk + off, walks)), device_id_type=pl.DeviceIdType.MESH)
    for off in range(1, ring):
        pl.semaphore_signal(barrier, inc=1, device_id=(lax.rem(me + off, ring), my_walk), device_id_type=pl.DeviceIdType.MESH)
    pl.semaphore_wait(barrier, walks + ring - 2)

    def hop(way, step, sub):
        owner = ring_dp(pos - step if way == 0 else pos + step, ring, high)
        block = held.at[pl.ds(owner * per_dev + (way * SUB + sub) * span, span)]
        return send(
            block, block, ring_send.at[way, step, sub], ring_recv.at[way, step, sub], nxt if way == 0 else prv, my_walk
        )

    hops = {}
    for way, sub in order:
        loads[way, sub].wait()
        for j in range((way * SUB + sub) * span, (way * SUB + sub + 1) * span):
            cols = slice(j * tile, (j + 1) * tile)
            rounded = wide[:, cols].astype(jnp.bfloat16)
            held[me * per_dev + j] = rounded
            own[:, cols] = rounded
        hops[way, 0, sub] = hop(way, 0, sub)
    mine = pltpu.make_async_copy(own, walk_ref.at[my_walk], local_sem.at[0])
    mine.start()
    sent = [
        send(own, walk_ref.at[my_walk], walk_send.at[off - 1], walk_recv.at[off - 1], me, lax.rem(my_walk + off, walks))
        for off in range(1, walks)
    ]
    held[ring * per_dev] = jnp.zeros((walkers, tile), jnp.bfloat16)
    sens_loads = []
    for n in range(CHUNKS):
        blocks = pl.ds(n * batch, batch)
        sens_loads.append(pltpu.make_async_copy(sens_ref.at[blocks], sens.at[blocks], sens_sem.at[n]))
        sens_loads[n].start()
    for step in range(1, ring - 1):
        for way, sub in [(way, sub) for sub in range(SUB) for way in range(2)]:
            hops[way, step - 1, sub].wait_recv()
            hops[way, step, sub] = hop(way, step, sub)
    for way, sub in order:
        hops[way, ring - 2, sub].wait_recv()
    for copy in sens_loads:
        copy.wait()

    def forward(n):
        def one_block(i, carry):
            blk = n * batch + i
            left, right = [], []
            for slot in range(slots):
                left.append(held[index_ref[blk, slot]])
                right.append(sens[blk, slot])
            total = lax.dot_general(
                jnp.concatenate(left, axis=1), jnp.concatenate(right, axis=1),
                (((1,), (1,)), ((), ())), preferred_element_type=jnp.float32,
            )
            cols = pl.ds(pl.multiple_of(i * tile, tile), tile)
            pred[n, :, cols] = total
            own_sums[n, :, cols] = jnp.sum(total, axis=0, keepdims=True)
            return carry

        lax.fori_loop(0, batch, one_block, 0)

    sent_sums, to_sibling, to_far, relays = {}, [], {}, {}

    def deviate(n):
        cols = slice(n * width, (n + 1) * width)
        total = own_sums[n]
        for off in range(1, walks):
            sent_sums[n, off].wait_recv()
            total = total + sums[n, off - 1]
        mean = total / WALKERS
        devs[n, my_walk] = (pred[n] - mean).astype(jnp.bfloat16)
        block = devs.at[n, my_walk]
        for off in range(1, far):
            other = lax.rem(my_far + off, far) * 2 + core
            to_far[n, off] = send(block, block, far_send.at[off - 1, n], far_recv.at[off - 1, n], me, other)
        to_sibling.append(send(block, block, sib_send.at[n], sib_recv.at[n], me, sibling))
        mis[n] = (prec_ref[:, cols] * (pred[n] - obs_ref[:, cols])).astype(jnp.bfloat16)

    for n in range(CHUNKS):
        forward(n)
        for off in range(1, walks):
            sent_sums[n, off] = send(
                own_sums.at[n], sums.at[n, off - 1], sum_send.at[off - 1, n], sum_recv.at[off - 1, n],
                me, lax.rem(my_walk + off, walks),
            )
        if n > 0:
            deviate(n - 1)
    deviate(CHUNKS - 1)

    def couple(n):
        to_sibling[n].wait_recv()
        for off in range(1, far):
            relays[n, off].wait_recv()
        every = devs[n].reshape(walks * walkers, width)
        product = lax.dot_general(mis[n], every, (((1,), (1,)), ((), ())), preferred_element_type=jnp.float32)
        acc[...] = product if n == 0 else acc[...] + product

    for n in range(CHUNKS):
        for off in range(1, far):
            to_far[n, off].wait_recv()
            origin = lax.rem(my_far + far - off, far) * 2 + core
            block = devs.at[n, origin]
            relays[n, off] = send(block, block, relay_send.at[off - 1, n], relay_recv.at[off - 1, n], me, sibling)
        if n > 0:
            couple(n - 1)
    couple(CHUNKS - 1)

    for d in range(ring):
        part[d] = acc[d * piece : (d + 1) * piece, :]
    sent_parts = []
    for off in range(1, ring):
        other = lax.rem(me + off, ring)
        sent_parts.append(
            send(part.at[other], parts_in.at[off - 1], part_send.at[off - 1], part_recv.at[off - 1], other, my_walk)
        )
    whole = part[me]
    for off in range(1, ring):
        sent_parts[off - 1].wait_recv()
        whole = whole + parts_in[off - 1]
    coup[me] = whole / WALKERS
    sent_coup = [
        send(coup.at[me], coup.at[me], coup_send.at[off - 1], coup_recv.at[off - 1], lax.rem(me + off, ring), my_walk)
        for off in range(1, ring)
    ]
    for copy in sent_coup:
        copy.wait_recv()
    coupling = jnp.concatenate([coup[d] for d in range(ring)], axis=0)
    sq_own[...] = jnp.sum(coupling * coupling, axis=0, keepdims=True)
    sent_sq = [
        send(sq_own, sq_in.at[off - 1], sq_send.at[off - 1], sq_recv.at[off - 1], me, lax.rem(my_walk + off, walks))
        for off in range(1, walks)
    ]
    squares = sq_own[...]
    for off in range(1, walks):
        sent_sq[off - 1].wait_recv()
        squares = squares + sq_in[off - 1]
    spread = jnp.sqrt(jnp.sum(squares, axis=1, keepdims=True) / (WALKERS * WALKERS) + 1e-06)
    out_ref[...] = (8.0 * coupling / (WALKERS * spread)).astype(jnp.bfloat16)
    for copies in (hops, sent_sums, to_far, relays):
        for copy in copies.values():
            copy.wait_send()
    for copy in to_sibling + sent_parts + sent_coup + sent_sq:
        copy.wait_send()
    for copy in sent:
        copy.wait()
    mine.wait()


def weigh(fields, sensitivity, tile_index, tile_count, observed, precision, ring, walks):
    walkers, cells = fields.shape
    nblocks, slots, tile, _ = sensitivity.shape
    rows = nblocks * tile
    width = rows // CHUNKS
    piece = walkers // ring
    far = walks // 2
    dma = pltpu.SemaphoreType.DMA
    vmem, anywhere, smem = (pl.BlockSpec(memory_space=m) for m in (pltpu.VMEM, pl.ANY, pltpu.SMEM))
    live = jnp.arange(slots)[None, :] < tile_count[:, None]
    index = jnp.where(live, tile_index, ring * (cells // tile))
    return pl.pallas_call(
        functools.partial(step_kernel, ring, HIGH, walks),
        out_shape=(
            jax.ShapeDtypeStruct((walkers, WALKERS), jnp.bfloat16),
            jax.ShapeDtypeStruct((walks, walkers, cells), jnp.bfloat16),
        ),
        in_specs=[smem, anywhere, anywhere, vmem, vmem],
        out_specs=(vmem, anywhere),
        scratch_shapes=[
            pltpu.VMEM((walkers, cells), jnp.float32),
            pltpu.VMEM((walkers, cells), jnp.bfloat16),
            pltpu.VMEM((ring * (cells // tile) + 1, walkers, tile), jnp.bfloat16),
            pltpu.VMEM((nblocks, slots, tile, tile), jnp.bfloat16),
            pltpu.VMEM((CHUNKS, walkers, width), jnp.float32),
            pltpu.VMEM((CHUNKS, 1, width), jnp.float32),
            pltpu.VMEM((CHUNKS, walks - 1, 1, width), jnp.float32),
            pltpu.VMEM((CHUNKS, walkers, width), jnp.bfloat16),
            pltpu.VMEM((CHUNKS, walks, walkers, width), jnp.bfloat16),
            pltpu.VMEM((walkers, WALKERS), jnp.float32),
            pltpu.VMEM((ring, piece, WALKERS), jnp.float32),
            pltpu.VMEM((ring - 1, piece, WALKERS), jnp.float32),
            pltpu.VMEM((ring, piece, WALKERS), jnp.float32),
            pltpu.VMEM((1, WALKERS), jnp.float32),
            pltpu.VMEM((walks - 1, 1, WALKERS), jnp.float32),
            dma((2 * SUB,)), dma((CHUNKS,)), dma((1,)),
            dma((2, ring - 1, SUB)), dma((2, ring - 1, SUB)),
            dma((walks - 1,)), dma((walks - 1,)),
            dma((walks - 1, CHUNKS)), dma((walks - 1, CHUNKS)),
            dma((CHUNKS,)), dma((CHUNKS,)),
            dma((far - 1, CHUNKS)), dma((far - 1, CHUNKS)),
            dma((far - 1, CHUNKS)), dma((far - 1, CHUNKS)),
            dma((ring - 1,)), dma((ring - 1,)),
            dma((ring - 1,)), dma((ring - 1,)),
            dma((walks - 1,)), dma((walks - 1,)),
        ],
        compiler_params=pltpu.CompilerParams(collective_id=0, has_side_effects=True, vmem_limit_bytes=58 * 2**20),
        name="weigh_walkers",
    )(index, fields, sensitivity, observed[None], precision[None])


def local(ring, walks, fields, sensitivity, tile_index, tile_count, observed, precision):
    weights, walk_fields = weigh(fields, sensitivity, tile_index, tile_count, observed, precision, ring, walks)
    update = jnp.dot(weights, walk_fields.reshape(WALKERS, -1), preferred_element_type=jnp.float32)
    return fields - update


def solution(mesh):
    placed = (P("walk", "dp"), P("dp", None, None, None), P("dp", None), P("dp"), P("dp"), P("dp"))
    return jax.shard_map(
        functools.partial(local, mesh.shape["dp"], mesh.shape["walk"]),
        mesh=mesh, in_specs=placed, out_specs=P("walk", "dp"), check_vma=False,
    )
```

time: 635 us -> 225 us (0.35)
  waiting for transfers between devices: 385 us -> 0 us
  Pallas kernels: 0 us -> 216 us
  local copies, waits for them, and re-layouts: 133 us -> 0.77 us
  matrix products: 53.6 us -> 6.76 us
  other arithmetic: 18.3 us -> 1.33 us
  blocking collectives: 16.7 us -> 0 us
  between operations: 13.8 us -> 0.02 us
  loops' own time: 11 us -> 0 us
    all_gather x3 -> x0, waiting for transfers between devices: 315 us -> none  [the longest x1 230 us: local(): gathered = lax.all_gather(field_bf, 'dp', axis=1, tiled=True)]
    pallas_call x0 -> x1, Pallas kernels: none -> 216 us  [weigh(): pl.pallas_call(functools.partial(step_kernel, ring, HIGH, walks), out_sha...]
    gather x16 -> x0, local copies, waits for them, and re-layouts: 104 us -> none  [one_slot(): blocks = jnp.take(cell_blocks, columns, axis=1)]
    psum x1 -> x0, waiting for transfers between devices: 70.1 us -> none  [local(): coupling_mine = lax.psum(partial_rows, 'dp') / WALKERS]
    dot_general x18 -> x1, matrix products: 53.6 us -> 6.76 us  [local(): jnp.dot(weights, walk_fields.reshape(WALKERS, -1), preferred_element_type...]
    while x2 -> x0, local copies, waits for them, and re-layouts: 24.3 us -> none  [forward(): totals = lax.fori_loop(0, most_live, one_slot, start_sum)]
    psum x2 -> x0, blocking collectives: 16.7 us -> none  [the longest x1 10.5 us: local(): pred_sum = lax.psum(jnp.sum(predicted, axis=0), 'walk')]
    reduce_and x16 -> x0, other arithmetic: 11.2 us -> none  [one_slot(): blocks = jnp.take(cell_blocks, columns, axis=1)]
  transfers between devices with their start and end apart: 4 -> 0, of which waited for: 4 -> 0; matrix products, arithmetic and copies ran while one was open for 0% -> 0% of each run, Pallas kernels for 0% -> 0%
where the time goes in v3:
time: 225 us
  Pallas kernels  216 us (96%)
  matrix products  6.76 us (3%)
    pallas_call x1, Pallas kernels, weigh(): pl.pallas_call(functools.partial(step_kernel, ring, HIGH, walks), out_sha...  216 us
    dot_general x1, matrix products, local(): jnp.dot(weights, walk_fields.reshape(WALKERS, -1), preferred_element_type...  6.76 us

profile of v3, /device:TPU:0, one launch (start us, length us, event | category | flops | bytes accessed | tf_op | source)
XLA Modules:
  0.0 224.9 jit_solution(7390107642912758651)
XLA Ops:
  0.0 0.8 copy.7
  0.8 1.3 fusion.index_ref
  2.1 0.0 copy-start
  2.1 216.0 %weigh_walkers.1 = (bf16[128,512]{1,0:T(8,128)(2,1)}, bf16[4,128,8192]{2,1,0:T(8,128)(2,1)}) custom-call(s32[32,16]{1,0:T(8,128)} %fusion.index_ref, f32[128,8192]{1,0:T(8,128)} %fields_ref.1, bf16[32,16,128,128]{3,2,1,0:T(8,128)(2,1)} %sens_ref.1, f32[1,4096]{1,0:T(1,128)} %bitcast.6, f32[1,4096]{1,0:T(1,128)} %bitcast.7), custom_call_target="tpu_custom_call" | custom-call | tf_op jit(solution)/shard_map/weigh_walkers/pallas_call | solution.py:227
  218.1 0.0 copy-done
  218.1 6.8 %convolution_subtract_fusion = f32[128,8192]{1,0:T(8,128)} fusion(f32[128,8192]{1,0:T(8,128)S(1)} %copy-done, bf16[128,512]{1,0:T(8,128)(2,1)} %get-tuple-element.7, bf16[512,8192]{1,0:T(8,128)(2,1)} %bitcast.5), kind=kOutput, calls=%fused_computation | convolution fusion | flops 1074790400 | bytes 16908288 | tf_op jit(solution)/shard_map/dot_general | solution.py:269
Async XLA Ops:
  2.1 216.0 %copy-start = (f32[128,8192]{1,0:T(8,128)S(1)}, f32[128,8192]{1,0:T(8,128)}, u32[]{:S(2)}) copy-start(f32[128,8192]{1,0:T(8,128)} %fields_ref.1) | copy-start | bytes 12582916

commit v4 on v3

--- a/solution.py
+++ b/solution.py
@@ -9,7 +9,7 @@
 
 WALKERS = 512
 SUB = 2
-CHUNKS = 4
+CHUNKS = 8
 HIGH = 4
 
 

time: 225 us -> 224 us (level)
  no operation moved by 1% of the time
where the time goes in v4:
time: 224 us
  Pallas kernels  215 us (96%)
  matrix products  6.76 us (3%)
    pallas_call x1, Pallas kernels, weigh(): pl.pallas_call(functools.partial(step_kernel, ring, HIGH, walks), out_sha...  215 us
    dot_general x1, matrix products, local(): jnp.dot(weights, walk_fields.reshape(WALKERS, -1), preferred_element_type...  6.76 us

profile of v4, /device:TPU:0, one launch (start us, length us, event | category | flops | bytes accessed | tf_op | source)
XLA Modules:
  0.0 223.9 jit_solution(16514137551772124032)
XLA Ops:
  0.0 0.8 copy.7
  0.8 1.3 fusion.index_ref
  2.1 0.0 copy-start
  2.1 215.0 %weigh_walkers.1 = (bf16[128,512]{1,0:T(8,128)(2,1)}, bf16[4,128,8192]{2,1,0:T(8,128)(2,1)}) custom-call(s32[32,16]{1,0:T(8,128)} %fusion.index_ref, f32[128,8192]{1,0:T(8,128)} %fields_ref.1, bf16[32,16,128,128]{3,2,1,0:T(8,128)(2,1)} %sens_ref.1, f32[1,4096]{1,0:T(1,128)} %bitcast.6, f32[1,4096]{1,0:T(1,128)} %bitcast.7), custom_call_target="tpu_custom_call" | custom-call | tf_op jit(solution)/shard_map/weigh_walkers/pallas_call | solution.py:227
  217.1 0.0 copy-done
  217.1 6.8 %convolution_subtract_fusion = f32[128,8192]{1,0:T(8,128)} fusion(f32[128,8192]{1,0:T(8,128)S(1)} %copy-done, bf16[128,512]{1,0:T(8,128)(2,1)} %get-tuple-element.7, bf16[512,8192]{1,0:T(8,128)(2,1)} %bitcast.5), kind=kOutput, calls=%fused_computation | convolution fusion | flops 1074790400 | bytes 16908288 | tf_op jit(solution)/shard_map/dot_general | solution.py:269
Async XLA Ops:
  2.1 215.0 %copy-start = (f32[128,8192]{1,0:T(8,128)S(1)}, f32[128,8192]{1,0:T(8,128)}, u32[]{:S(2)}) copy-start(f32[128,8192]{1,0:T(8,128)} %fields_ref.1) | copy-start | bytes 12582916
